TPU v7x, 32 devices: a whole 2x2x4 slice. The times are simulated.
32 devices in a mesh: tile: 8 (over z, y), lev: 4 (over x, core).
Axes of the slice: x: 2, y: 2, z: 4, core: 2. Of those that a mesh axis runs over, the one named last changes fastest.
Arguments:
- cotangent: bfloat16 [3072, 128, 128], P('lev', 'tile'), may hold values from -6 to 6
- mix_weight: bfloat16 [3072, 3072], P(None, 'tile'), may hold values from -0.109375 to 0.109375
- kernel: float32 [3072, 9], P('lev'), may hold values from -2 to 2
- send_rows: int32 [8, 8, 41], P('tile'), may hold values from -1 to 291, as said below
- recv_cells: int32 [8, 8, 41], P('tile'), may hold values from -1 to 1918, as said below
- recv_weight: float32 [8, 4, 8, 41], P('tile'), may hold values from 0 to 1, as said below
Outputs:
- grad_input: bfloat16 [3072, 128, 128], P('lev', 'tile')
Inputs may be any that keep to these rules, and one draw needn't show every extreme that they name: `send_rows`: partner d is always a strip of the other panel. Every slot of the side columns (with the four corners) of strip s appears exactly once over all d and k, the slots of row 0 only for the strip at place 0 of a panel and those of row 17 only for the strip at place 4 - 1; no other slots appear. Used entries of a block come first, and some pair uses all 41. recv_cells[d, s, k] is -1 exactly where send_rows[s, d, k] is -1; otherwise its row is at most 14 and its column at most 126, so all four corners lie in strip d; the largest cell is reached. `recv_weight`: the four weights of an entry are the bilinear weights of a point in the donor cell and sum to one.
All inputs are finite; a program needn't handle non-finite values.
Results may differ from a plain program's by a relative error of at most 0.0049.
Values may be sent and summed in bfloat16 or wider, within the bound.
A program may use at most 128 MiB of HBM per device.

v0:
```python
import jax
import jax.numpy as jnp
from jax import lax
from jax.sharding import PartitionSpec as P


def padded_2(cells, sides, width):
    for axis, dim in sides:
        count = lax.axis_size(axis)
        head = lax.slice_in_dim(cells, 0, width, axis=dim)
        tail = lax.slice_in_dim(cells, cells.shape[dim] - width, cells.shape[dim], axis=dim)
        cells = jnp.concatenate(
            [
                lax.ppermute(tail, axis, [(i, (i + 1) % count) for i in range(count)]),
                cells,
                lax.ppermute(head, axis, [((i + 1) % count, i) for i in range(count)]),
            ],
            axis=dim,
        )
    return cells


def stencil_adjoint(grad_block, kernel):
    feat_local, tile_rows, tile_cols = grad_block.shape
    padded = jnp.pad(grad_block.astype(jnp.float32), ((0, 0), (2, 2), (2, 2)))
    summed = jnp.zeros((feat_local, tile_rows + 2, tile_cols + 2), jnp.float32)
    for row_shift in (-1, 0, 1):
        for col_shift in (-1, 0, 1):
            kernel_tap = kernel[:, 3 * (row_shift + 1) + col_shift + 1]
            window_part = padded[
                :,
                1 - row_shift : 3 - row_shift + tile_rows,
                1 - col_shift : 3 - col_shift + tile_cols,
            ]
            summed = summed + kernel_tap[:, None, None] * window_part
    return summed


def cycle_of(extended):
    return jnp.concatenate(
        [extended[:, 0, :], extended[:, -1, :], extended[:, 1:-1, 0], extended[:, 1:-1, -1]], axis=1
    )


def deposit(running, values, cell_index, weight_rows, row_length):
    is_used = cell_index >= 0
    base_cell = jnp.maximum(cell_index, 0)
    spread = values.astype(jnp.float32)
    for corner, offset in enumerate((0, 1, row_length, row_length + 1)):
        running = running.at[:, base_cell + offset].add(
            spread * jnp.where(is_used, weight_rows[corner], 0.0)[None, :]
        )
    return running


def per_device(cotangent, mix_weight, kernel, send_rows, recv_cells, recv_weight):
    feat_local, tile_rows, tile_cols = cotangent.shape
    cell_count = tile_rows * tile_cols
    flat_grad = cotangent.reshape(feat_local, cell_count)
    level_index = lax.axis_index("lev")
    own_rows = lax.dynamic_slice_in_dim(mix_weight, level_index * feat_local, feat_local, 0)
    weight_rows = lax.all_gather(own_rows, "tile", axis=1, tiled=True)
    grad_mix = jnp.dot(
        weight_rows,
        lax.all_gather(flat_grad, "lev", axis=0, tiled=True),
        preferred_element_type=jnp.float32,
    ).astype(jnp.bfloat16)
    extended = stencil_adjoint(grad_mix.reshape(feat_local, tile_rows, tile_cols), kernel)
    cycle_values = cycle_of(extended).astype(jnp.bfloat16)
    tile_count = lax.axis_size("tile")
    strip_count = tile_count // 2
    tile_here = lax.axis_index("tile")
    place_index = (tile_here + strip_count // 2) % tile_count % strip_count
    keep_top = (place_index != 0).astype(jnp.float32)
    keep_bottom = (place_index != strip_count - 1).astype(jnp.float32)
    edge_rows = jnp.stack(
        [extended[:, 0, 1:-1] * keep_top, extended[:, -1, 1:-1] * keep_bottom], axis=1
    )
    bordered = padded_2(edge_rows.astype(jnp.bfloat16), (("tile", 1),), 1).astype(edge_rows.dtype)
    interior = extended[:, 1:-1, 1:-1]
    interior = interior.at[:, 0, :].add(bordered[:, 0, :]).at[:, -1, :].add(bordered[:, 3, :])
    running = interior.reshape(feat_local, cell_count)
    cell_lists = recv_cells[0]
    weight_lists = recv_weight[0]
    slot_lists = lax.all_to_all(send_rows[0], "tile", split_axis=0, concat_axis=0, tiled=True)
    cycle_size = cycle_values.shape[1]
    shard_piece = lax.all_gather(cycle_values, "tile", axis=1, tiled=True)
    sources = shard_piece.shape[1] // cycle_size
    local_slots = (
        jnp.arange(sources, dtype=jnp.int32)[:, None] * cycle_size + jnp.maximum(slot_lists, 0)
    ).reshape(-1)
    values = jnp.take(shard_piece, local_slots, axis=1)
    cells_part = cell_lists.reshape(-1)
    weights_part = weight_lists.reshape(4, -1)
    running = deposit(running, values, cells_part, weights_part, tile_cols)
    return running.reshape(feat_local, tile_rows, tile_cols).astype(jnp.bfloat16)


def solution(mesh):
    in_specs = (
        P("lev", "tile", None),
        P(None, "tile"),
        P("lev", None),
        P("tile", None, None),
        P("tile", None, None),
        P("tile", None, None, None),
    )
    out_specs = P("lev", "tile", None)
    return jax.shard_map(
        per_device, mesh=mesh, in_specs=in_specs, out_specs=out_specs, check_vma=False
    )
```

profile of v0, /device:TPU:0, one launch (start us, length us, event | category | flops | bytes accessed | tf_op | source)
XLA Modules:
  0.0 363.0 jit_solution(4709097112009996498)
XLA Ops:
  6.5 1.7 copy-done
  9.1 4.9 %copy.22 = bf16[96,8,16,128]{3,1,2,0:T(8,128)(2,1)} copy(bf16[96,8,16,128]{3,2,1,0:T(8,128)(2,1)} %bitcast.36) | data formatting | bytes 6291456
  14.2 79.0 %all-gather.5.cloned.1.call-done = bf16[768,3072]{1,0:T(8,128)(2,1)} async-done(((bf16[768,384]{1,0:T(8,128)(2,1)}), bf16[768,3072]{1,0:T(8,128)(2,1)}) %all-gather.5.cloned.1.call-update) | async-done | bytes 4718608 | tf_op jit(solution)/shard_map/all_gather | solution.py:62
  93.2 81.9 %all-gather.7.cloned.1.call-done = bf16[3072,2048]{1,0:T(8,128)(2,1)} async-done(((bf16[768,2048]{1,0:T(8,128)(2,1)}), bf16[3072,2048]{1,0:T(8,128)(2,1)}) %all-gather.7.cloned.1.call-update) | async-done | bytes 12582928 | tf_op jit(solution)/shard_map/all_gather | solution.py:65
  175.0 15.4 %convolution_convert_fusion = bf16[768,2048]{1,0:T(8,128)(2,1)} fusion(bf16[768,3072]{1,0:T(8,128)(2,1)} %all-gather.5.cloned.1.call-done, bf16[3072,2048]{1,0:T(8,128)(2,1)} %all-gather.7.cloned.1.call-done), kind=kOutput, calls=%fused_computation.23 | convolution fusion | flops 9665249280 | bytes 20447232 | tf_op jit(solution)/shard_map/dot_general | solution.py:63
  190.4 4.7 %copy.15 = bf16[768,2048]{0,1:T(8,128)(2,1)} copy(bf16[768,2048]{1,0:T(8,128)(2,1)} %convolution_convert_fusion) | data formatting | bytes 6291456 | tf_op jit(solution)/shard_map/convert_element_type | solution.py:25
  195.1 5.8 %pad_convert_fusion = f32[768,20,132]{0,2,1:T(8,128)} fusion(bf16[768,16,128]{0,2,1:T(8,128)(2,1)} %bitcast.34), kind=kLoop, calls=%fused_computation.22 | loop fusion | flops 2027520 | bytes 11255808 | tf_op jit(solution)/shard_map/jit(_pad)/pad | solution.py:25
  200.9 28.3 %fusion.25 = (bf16[768,18,130]{0,2,1:T(8,128)(2,1)}, f32[768,18,130]{0,2,1:T(8,128)}) fusion(f32[768,20,132]{0,2,1:T(8,128)} %pad_convert_fusion, f32[768]{0:T(1024)S(1)} %get-tuple-element.36, f32[768]{0:T(1024)S(1)} %get-tuple-element.37, f32[768]{0:T(1024)S(1)} %get-tuple-element.30, f32[768]{0:T(1024)S(1)} %get-tuple-element.31, ...), kind=kLoop, calls=%fused_computation.90 | loop fusion | flops 32348160 | bytes 75506688 | tf_op jit(solution)/shard_map/convert.14
  232.3 5.5 %all-to-all-start = ((s32[8,1,41]{2,1,0:T(1,128)}), s32[8,1,41]{2,1,0:T(1,128)S(1)}, u32[]{:S(2)}, u32[]{:S(2)}) async-start(s32[8,1,41]{2,1,0:T(1,128)} %bitcast.2), calls=%async_computation | async-start | bytes 8192 | tf_op jit(solution)/shard_map/all_to_all | solution.py:85
  239.2 5.0 %all-to-all-done = s32[8,1,41]{2,1,0:T(1,128)S(1)} async-done(((s32[8,1,41]{2,1,0:T(1,128)}), s32[8,1,41]{2,1,0:T(1,128)S(1)}, u32[]{:S(2)}, u32[]{:S(2)}) %all-to-all-start) | async-done | bytes 1344 | tf_op jit(solution)/shard_map/all_to_all | solution.py:85
  246.2 4.2 %collective-permute-start.1 = (bf16[768,1,128]{0,2,1:T(8,128)(2,1)S(1)}, bf16[768,1,128]{0,2,1:T(8,128)(2,1)S(1)}, u32[]{:S(2)}, u32[]{:S(2)}) collective-permute-start(bf16[768,1,128]{0,2,1:T(8,128)(2,1)S(1)} %get-tuple-element.41), channel_id=1, source_target_pairs={{4,0},{8,4},{12,8},{16,12},{20,16},{24,20},{28,24},{0,28},{5,1},{9... | collective-permute-start | bytes 589832 | tf_op jit(solution)/shard_map/ppermute | solution.py:16
  250.4 6.3 %slice.198 = f32[768,16,128]{0,2,1:T(8,128)} slice(f32[768,18,130]{0,2,1:T(8,128)} %get-tuple-element.39), slice={[0:768], [1:17], [1:129]} | slice | bytes 12582912 | tf_op jit(solution)/shard_map/slice | solution.py:80
  256.7 2.9 collective-permute-done
  259.6 1.8 fusion.17
  261.4 1.8 fusion.16
  263.2 40.2 %all-gather.9.cloned.1.call-done = bf16[8,292,768]{2,1,0:T(8,128)(2,1)} async-done(((bf16[1,292,768]{2,1,0:T(8,128)(2,1)}), bf16[8,292,768]{2,1,0:T(8,128)(2,1)}) %all-gather.9.cloned.1.call-update) | async-done | bytes 3588112 | tf_op jit(solution)/shard_map/all_gather | solution.py:87
  303.4 4.7 %reshape.290 = bf16[2336,768]{1,0:T(8,128)(2,1)} reshape(bf16[8,292,768]{2,1,0:T(8,128)(2,1)} %all-gather.9.cloned.1.call-done) | data formatting | bytes 7176192
  308.1 5.0 %gather_fusion = bf16[328,768]{1,0:T(8,128)(2,1)S(1)} fusion(bf16[768,2336]{0,1:T(8,128)(2,1)} %bitcast.32, s32[1024]{0:T(1024)S(1)} %pad_clamp_fusion), kind=kCustom, calls=%fused_computation | custom fusion | bytes 1008928 | tf_op jit(solution)/shard_map/jit(_take)/gather | solution.py:92
  313.1 8.4 %scatter_custom_fusion = f32[768,2048]{0,1:T(8,128)} fusion(f32[768,2048]{0,1:T(8,128)} %bitcast.1, s32[328]{0:T(512)S(1)} %reshape.246, f32[328]{0:T(512)S(1)} %get-tuple-element.62, bf16[328,768]{1,0:T(8,128)(2,1)S(1)} %gather_fusion, pred[328]{0:T(512)(128)(4,1)S(1)} %compare_and_fusion), kind=kCustom, calls=%fused_computation.30 | custom fusion | flops 1007616 | bytes 6797824 | tf_op jit(solution)/shard_map/scatter-add | solution.py:50
  321.4 8.4 %scatter_custom_fusion.1 = f32[768,2048]{0,1:T(8,128)} fusion(f32[768,2048]{0,1:T(8,128)} %scatter_custom_fusion, s32[328]{0:T(512)S(1)} %fusion.21, f32[328]{0:T(512)S(1)} %get-tuple-element.61, bf16[328,768]{1,0:T(8,128)(2,1)S(1)} %gather_fusion, pred[328]{0:T(512)(128)(4,1)S(1)} %compare_and_fusion), kind=kCustom, calls=%fused_computation.31 | custom fusion | flops 1007616 | bytes 6797824 | tf_op jit(solution)/shard_map/scatter-add | solution.py:50
  329.8 8.4 %scatter_custom_fusion.2 = f32[768,2048]{0,1:T(8,128)} fusion(f32[768,2048]{0,1:T(8,128)} %scatter_custom_fusion.1, s32[328]{0:T(512)S(1)} %fusion.22, f32[328]{0:T(512)S(1)} %get-tuple-element.60, bf16[328,768]{1,0:T(8,128)(2,1)S(1)} %gather_fusion, pred[328]{0:T(512)(128)(4,1)S(1)} %compare_and_fusion), kind=kCustom, calls=%fused_computation.32 | custom fusion | flops 1007616 | bytes 6797824 | tf_op jit(solution)/shard_map/scatter-add | solution.py:50
  338.2 8.5 %scatter_custom_fusion.3 = f32[768,2048]{0,1:T(8,128)} fusion(f32[768,2048]{0,1:T(8,128)} %scatter_custom_fusion.2, s32[328]{0:T(512)S(1)} %fusion.23, f32[328]{0:T(512)S(1)} %get-tuple-element.59, bf16[328,768]{1,0:T(8,128)(2,1)S(1)} %gather_fusion, pred[328]{0:T(512)(128)(4,1)S(1)} %compare_and_fusion), kind=kCustom, calls=%fused_computation.29 | custom fusion | flops 1007616 | bytes 6797824 | tf_op jit(solution)/shard_map/scatter-add | solution.py:50
  346.7 4.8 %convert_element_type.35 = bf16[768,2048]{0,1:T(8,128)(2,1)} convert(f32[768,2048]{0,1:T(8,128)} %scatter_custom_fusion.3) | non-fusion elementwise | flops 1572864 | bytes 9437184 | tf_op jit(solution)/shard_map/convert_element_type | solution.py:96
  351.5 5.0 %copy.14 = bf16[768,16,128]{2,1,0:T(8,128)(2,1)} copy(bf16[768,16,128]{0,2,1:T(8,128)(2,1)} %bitcast.35) | data formatting | bytes 6291456 | tf_op jit(solution)/shard_map/convert_element_type | solution.py:96
  (53 shorter events, 7.4 us)
Async XLA Ops:
  6.5 1.7 copy-start
  6.5 7.5 %copy-start.4 = (f32[768,9]{0,1:T(8,128)S(1)}, f32[768,9]{0,1:T(8,128)}, u32[]{:S(2)}) copy-start(f32[768,9]{0,1:T(8,128)} %param.12) | copy-start | bytes 82948
  6.5 86.6 %all-gather.5.cloned.1.call-start = ((), (), s32[]{:S(2)}) async-start(), calls=%async_computation.1 | async-start | bytes 5308416 | tf_op jit(solution)/shard_map/all_gather | solution.py:62
  9.1 165.9 %all-gather.7.cloned.1.call-start = ((), (), s32[]{:S(2)}) async-start(), calls=%async_computation.2 | async-start | bytes 15728640 | tf_op jit(solution)/shard_map/all_gather | solution.py:65
  14.0 289.4 %all-gather.9.cloned.1.call-start = ((), (), s32[]{:S(2)}) async-start(), calls=%async_computation.3 | async-start | bytes 4091904 | tf_op jit(solution)/shard_map/all_gather | solution.py:87
  200.9 36.8 %copy-start.2 = (f32[1,4,8,41]{3,2,1,0:T(8,128)S(1)}, f32[1,4,8,41]{3,2,1,0:T(8,128)}, u32[]{:S(2)}) copy-start(f32[1,4,8,41]{3,2,1,0:T(8,128)} %param.15) | copy-start | bytes 15748
  200.9 37.2 %copy-start.3 = (s32[1,8,41]{2,1,0:T(8,128)S(1)}, s32[1,8,41]{2,1,0:T(8,128)}, u32[]{:S(2)}) copy-start(s32[1,8,41]{2,1,0:T(8,128)} %param.14) | copy-start | bytes 3940
  232.3 11.9 %all-to-all-start = ((s32[8,1,41]{2,1,0:T(1,128)}), s32[8,1,41]{2,1,0:T(1,128)S(1)}, u32[]{:S(2)}, u32[]{:S(2)}) async-start(s32[8,1,41]{2,1,0:T(1,128)} %bitcast.2), calls=%async_computation | async-start | bytes 8192 | tf_op jit(solution)/shard_map/all_to_all | solution.py:85
  245.6 14.0 %collective-permute-start = (bf16[768,1,128]{0,2,1:T(8,128)(2,1)S(1)}, bf16[768,1,128]{0,2,1:T(8,128)(2,1)S(1)}, u32[]{:S(2)}, u32[]{:S(2)}) collective-permute-start(bf16[768,1,128]{0,2,1:T(8,128)(2,1)S(1)} %get-tuple-element.40), channel_id=1, source_target_pairs={{0,4},{4,8},{8,12},{12,16},{16,20},{20,24},{24,28},{28,0},{1,5},{5... | collective-permute-start | bytes 589832 | tf_op jit(solution)/shard_map/ppermute | solution.py:14
  246.2 13.4 %collective-permute-start.1 = (bf16[768,1,128]{0,2,1:T(8,128)(2,1)S(1)}, bf16[768,1,128]{0,2,1:T(8,128)(2,1)S(1)}, u32[]{:S(2)}, u32[]{:S(2)}) collective-permute-start(bf16[768,1,128]{0,2,1:T(8,128)(2,1)S(1)} %get-tuple-element.41), channel_id=1, source_target_pairs={{4,0},{8,4},{12,8},{16,12},{20,16},{24,20},{28,24},{0,28},{5,1},{9... | collective-permute-start | bytes 589832 | tf_op jit(solution)/shard_map/ppermute | solution.py:16
  338.2 18.3 %copy-start.1 = (bf16[3072,384]{1,0:T(8,128)(2,1)S(1)}, bf16[3072,384]{1,0:T(8,128)(2,1)}, u32[]{:S(2)}) copy-start(bf16[3072,384]{1,0:T(8,128)(2,1)} %param.11) | copy-start | bytes 7077892
Sparse Core Ops, SparseCore 0:
  9.4 83.6 all-gather.4
  94.7 80.2 all-gather.6
  232.4 70.9 all-gather.8
where the time goes:
time: 364 us; the launch traced here: 363 us
  waiting for transfers between devices  209 us (57%)
  other arithmetic  78.3 us (22%)
  local copies, waits for them, and re-layouts  36.6 us (10%)
  matrix products  15.4 us (4%)
  between operations  13.3 us (4%)
  starting transfers between devices  10.4 us (3%)
    all_gather x1, waiting for transfers between devices, per_device(): lax.all_gather(flat_grad, 'lev', axis=0, tiled=True)  81.9 us
    all_gather x1, waiting for transfers between devices, per_device(): weight_rows = lax.all_gather(own_rows, 'tile', axis=1, tiled=True)  79 us
    all_gather x1, waiting for transfers between devices, per_device(): shard_piece = lax.all_gather(cycle_values, 'tile', axis=1, tiled=True)  40.2 us
    scatter-add x4, other arithmetic, deposit(): running.at[:, base_cell + offset]  33.6 us
    another operation x1, other arithmetic  28.3 us
    dot_general x1, matrix products, per_device(): jnp.dot(weight_rows, lax.all_gather(flat_grad, 'lev', axis=0, tiled=True)...  15.4 us
    unnamed x13, local copies, waits for them, and re-layouts  11.3 us
  transfers between devices with their start and end apart: 6, of which 5 were waited for; matrix products, arithmetic and copies ran while one was open for 5% of the time, Pallas kernels for 0%

commit v1 on v0

--- a/solution.py
+++ b/solution.py
@@ -2,6 +2,28 @@
 import jax.numpy as jnp
 from jax import lax
 from jax.sharding import PartitionSpec as P
+
+
+def laid_out(pieces, dim):
+    pieces = jnp.moveaxis(pieces, 0, dim)
+    shape = pieces.shape
+    return pieces.reshape(*shape[:dim], shape[dim] * shape[dim + 1], *shape[dim + 2 :])
+
+
+def collect(value, axis, dim):
+    size = lax.axis_size(axis)
+    pairs = [(i, (i + 1) % size) for i in range(size)]
+    back = [(b, a) for a, b in pairs]
+    lower, upper = ([], [])
+    for step in range(size - 1):
+        if step % 2 == 0:
+            lower.append(lax.ppermute(lower[-1] if lower else value, axis, pairs))
+        else:
+            upper.append(lax.ppermute(upper[-1] if upper else value, axis, back))
+    tiles = jnp.stack([*lower[::-1], value, *upper])
+    shift = lax.axis_index(axis) - len(lower)
+    tiles = tiles[(jnp.arange(size) - shift) % size]
+    return laid_out(tiles, dim)
 
 
 def padded_2(cells, sides, width):
@@ -84,7 +106,7 @@
     weight_lists = recv_weight[0]
     slot_lists = lax.all_to_all(send_rows[0], "tile", split_axis=0, concat_axis=0, tiled=True)
     cycle_size = cycle_values.shape[1]
-    shard_piece = lax.all_gather(cycle_values, "tile", axis=1, tiled=True)
+    shard_piece = collect(cycle_values, "tile", 1)
     sources = shard_piece.shape[1] // cycle_size
     local_slots = (
         jnp.arange(sources, dtype=jnp.int32)[:, None] * cycle_size + jnp.maximum(slot_lists, 0)

time: 364 us -> 386 us (1.060)
  starting transfers between devices: 10.4 us -> 26.3 us
  local copies, waits for them, and re-layouts: 36.6 us -> 47.2 us
  waiting for transfers between devices: 209 us -> 205 us
    ppermute x0 -> x7, waiting for transfers between devices: none -> 50.7 us  [the longest x4 37.4 us: collect(): lower.append(lax.ppermute(lower[-1] if lower else value, axis, pairs))]
    all_gather x1 -> x0, waiting for transfers between devices: 40.2 us -> none  [per_device(): shard_piece = lax.all_gather(cycle_values, 'tile', axis=1, tiled=True)]
    another operation x1 -> x0, other arithmetic: 28.3 us -> none
    add x0 -> x1, other arithmetic: none -> 26.9 us  [stencil_adjoint(): summed = summed + kernel_tap[:, None, None] * window_part]
    ppermute x0 -> x7, starting transfers between devices: none -> 16.6 us  [the longest x3 10.1 us: collect(): upper.append(lax.ppermute(upper[-1] if upper else value, axis, back))]
    all_gather x1, waiting for transfers between devices: 79 us -> 70.8 us  [per_device(): weight_rows = lax.all_gather(own_rows, 'tile', axis=1, tiled=True)]
    all_to_all x1, waiting for transfers between devices: 5.02 us -> 0.01 us  [per_device(): lax.all_to_all(send_rows[0], 'tile', split_axis=0, concat_axis=0, tiled=T...]
    reshape x0 -> x1, local copies, waits for them, and re-layouts: none -> 4.71 us  [laid_out(): pieces.reshape(*shape[:dim], shape[dim] * shape[dim + 1], *shape[dim + 2:])]
  transfers between devices with their start and end apart: 6 -> 12, of which waited for: 5 -> 8; matrix products, arithmetic and copies ran while one was open for 5% -> 20% of each run, Pallas kernels for 0% -> 0%
where the time goes in v1:
time: 386 us; the launch traced here: 385 us
  waiting for transfers between devices  205 us (53%)
  other arithmetic  77 us (20%)
  local copies, waits for them, and re-layouts  47.2 us (12%)
  starting transfers between devices  26.3 us (7%)
  matrix products  15.4 us (4%)
  between operations  13.6 us (4%)
    all_gather x1, waiting for transfers between devices, per_device(): lax.all_gather(flat_grad, 'lev', axis=0, tiled=True)  81.9 us
    all_gather x1, waiting for transfers between devices, per_device(): weight_rows = lax.all_gather(own_rows, 'tile', axis=1, tiled=True)  70.8 us
    ppermute x4, waiting for transfers between devices, collect(): lower.append(lax.ppermute(lower[-1] if lower else value, axis, pairs))  37.4 us
    scatter-add x4, other arithmetic, deposit(): running.at[:, base_cell + offset]  33.6 us
    add x1, other arithmetic, stencil_adjoint(): summed = summed + kernel_tap[:, None, None] * window_part  26.9 us
    dot_general x1, matrix products, per_device(): jnp.dot(weight_rows, lax.all_gather(flat_grad, 'lev', axis=0, tiled=True)...  15.4 us
    ppermute x3, waiting for transfers between devices, collect(): upper.append(lax.ppermute(upper[-1] if upper else value, axis, back))  13.3 us
    unnamed x18, local copies, waits for them, and re-layouts  11.4 us
  transfers between devices with their start and end apart: 12, of which 8 were waited for; matrix products, arithmetic and copies ran while one was open for 20% of the time, Pallas kernels for 0%

profile of v1, /device:TPU:0, one launch (start us, length us, event | category | flops | bytes accessed | tf_op | source)
XLA Modules:
  0.0 384.6 jit_solution(13841306222062664544)
XLA Ops:
  9.1 4.9 %copy.26 = bf16[96,8,16,128]{3,1,2,0:T(8,128)(2,1)} copy(bf16[96,8,16,128]{3,2,1,0:T(8,128)(2,1)} %bitcast.58) | data formatting | bytes 6291456
  14.0 7.3 %all-to-all-start = ((s32[8,1,41]{2,1,0:T(1,128)}), s32[8,1,41]{2,1,0:T(1,128)S(1)}, u32[]{:S(2)}, u32[]{:S(2)}) async-start(s32[8,1,41]{2,1,0:T(1,128)} %bitcast.2), calls=%async_computation | async-start | bytes 8192 | tf_op jit(solution)/shard_map/all_to_all | solution.py:107
  22.4 70.8 %all-gather.3.cloned.1.call-done = bf16[768,3072]{1,0:T(8,128)(2,1)} async-done(((bf16[768,384]{1,0:T(8,128)(2,1)}), bf16[768,3072]{1,0:T(8,128)(2,1)}) %all-gather.3.cloned.1.call-update) | async-done | bytes 4718608 | tf_op jit(solution)/shard_map/all_gather | solution.py:84
  93.2 81.9 %all-gather.5.cloned.1.call-done = bf16[3072,2048]{1,0:T(8,128)(2,1)} async-done(((bf16[768,2048]{1,0:T(8,128)(2,1)}), bf16[3072,2048]{1,0:T(8,128)(2,1)}) %all-gather.5.cloned.1.call-update) | async-done | bytes 12582928 | tf_op jit(solution)/shard_map/all_gather | solution.py:87
  175.1 15.4 %convolution_convert_fusion = bf16[768,2048]{1,0:T(8,128)(2,1)} fusion(bf16[768,3072]{1,0:T(8,128)(2,1)} %all-gather.3.cloned.1.call-done, bf16[3072,2048]{1,0:T(8,128)(2,1)} %all-gather.5.cloned.1.call-done), kind=kOutput, calls=%fused_computation.24 | convolution fusion | flops 9665249280 | bytes 20447232 | tf_op jit(solution)/shard_map/dot_general | solution.py:85
  190.5 4.7 %copy.15 = bf16[768,2048]{0,1:T(8,128)(2,1)} copy(bf16[768,2048]{1,0:T(8,128)(2,1)} %convolution_convert_fusion) | data formatting | bytes 6291456 | tf_op jit(solution)/shard_map/convert_element_type | solution.py:47
  195.2 5.8 %pad_convert_fusion = f32[768,20,132]{0,2,1:T(8,128)} fusion(bf16[768,16,128]{0,2,1:T(8,128)(2,1)} %bitcast.56), kind=kLoop, calls=%fused_computation.23 | loop fusion | flops 2027520 | bytes 11255808 | tf_op jit(solution)/shard_map/jit(_pad)/pad | solution.py:47
  201.0 26.9 %fusion = f32[768,18,130]{0,2,1:T(8,128)} fusion(f32[768,20,132]{0,2,1:T(8,128)} %pad_convert_fusion, f32[768]{0:T(1024)S(1)} %get-tuple-element.36, f32[768]{0:T(1024)S(1)} %get-tuple-element.37, f32[768]{0:T(1024)S(1)} %get-tuple-element.30, f32[768]{0:T(1024)S(1)} %get-tuple-element.31, f32[768]{0:T(1024)S(1)} %get-tuple-element.32, ...), kind=kLoop, calls=%fused_computation.7 | loop fusion | flops 30551040 | bytes 71912448 | tf_op jit(solution)/shard_map/add | solution.py:57
  232.3 13.5 %collective-permute-done.2 = bf16[768,292]{0,1:T(8,128)(2,1)S(1)} collective-permute-done((bf16[768,292]{0,1:T(8,128)(2,1)S(1)}, bf16[768,292]{0,1:T(8,128)(2,1)S(1)}, u32[]{:S(2)}, u32[]{:S(2)}) %collective-permute-start.2) | collective-permute-done | bytes 448544 | tf_op jit(solution)/shard_map/ppermute | solution.py:20
  246.0 4.8 %collective-permute-start.6 = (bf16[768,292]{0,1:T(8,128)(2,1)S(1)}, bf16[768,292]{0,1:T(8,128)(2,1)S(1)}, u32[]{:S(2)}, u32[]{:S(2)}) collective-permute-start(bf16[768,292]{0,1:T(8,128)(2,1)S(1)} %pad_maximum_fusion), channel_id=1, source_target_pairs={{4,0},{8,4},{12,8},{16,12},{20,16},{24,20},{28,24},{0,28},{5,1},{9... | collective-permute-start | bytes 1345544 | tf_op jit(solution)/shard_map/ppermute | solution.py:22
  250.8 14.3 %collective-permute-done.3 = bf16[768,292]{0,1:T(8,128)(2,1)S(1)} collective-permute-done((bf16[768,292]{0,1:T(8,128)(2,1)S(1)}, bf16[768,292]{0,1:T(8,128)(2,1)S(1)}, u32[]{:S(2)}, u32[]{:S(2)}) %collective-permute-start.3) | collective-permute-done | bytes 448544 | tf_op jit(solution)/shard_map/ppermute | solution.py:20
  271.1 6.3 %slice.196 = f32[768,16,128]{0,2,1:T(8,128)} slice(f32[768,18,130]{0,2,1:T(8,128)} %fusion), slice={[0:768], [1:17], [1:129]} | slice | bytes 12582912 | tf_op jit(solution)/shard_map/slice | solution.py:102
  277.4 5.4 %collective-permute-start.7 = (bf16[768,292]{0,1:T(8,128)(2,1)S(1)}, bf16[768,292]{0,1:T(8,128)(2,1)S(1)}, u32[]{:S(2)}, u32[]{:S(2)}) collective-permute-start(bf16[768,292]{0,1:T(8,128)(2,1)S(1)} %collective-permute-done.6), channel_id=1, source_target_pairs={{4,0},{8,4},{12,8},{16,12},{20,16},{24,20},{28,24},{0,28},{5,1},{9... | collective-permute-start | bytes 1345544 | tf_op jit(solution)/shard_map/ppermute | solution.py:22
  282.7 9.7 %collective-permute-done.4 = bf16[768,292]{0,1:T(8,128)(2,1)S(1)} collective-permute-done((bf16[768,292]{0,1:T(8,128)(2,1)S(1)}, bf16[768,292]{0,1:T(8,128)(2,1)S(1)}, u32[]{:S(2)}, u32[]{:S(2)}) %collective-permute-start.4) | collective-permute-done | bytes 448544 | tf_op jit(solution)/shard_map/ppermute | solution.py:20
  300.2 6.7 %collective-permute-done.7 = bf16[768,292]{0,1:T(8,128)(2,1)S(1)} collective-permute-done((bf16[768,292]{0,1:T(8,128)(2,1)S(1)}, bf16[768,292]{0,1:T(8,128)(2,1)S(1)}, u32[]{:S(2)}, u32[]{:S(2)}) %collective-permute-start.7) | collective-permute-done | bytes 448544 | tf_op jit(solution)/shard_map/ppermute | solution.py:22
  312.6 6.6 %collective-permute-done.8 = bf16[768,292]{0,1:T(8,128)(2,1)S(1)} collective-permute-done((bf16[768,292]{0,1:T(8,128)(2,1)S(1)}, bf16[768,292]{0,1:T(8,128)(2,1)S(1)}, u32[]{:S(2)}, u32[]{:S(2)}) %collective-permute-start.8) | collective-permute-done | bytes 448544 | tf_op jit(solution)/shard_map/ppermute | solution.py:22
  324.7 4.7 %reshape.351 = bf16[768,2336]{0,1:T(8,128)(2,1)} reshape(bf16[768,8,292]{0,2,1:T(8,128)(2,1)} %bitcast.54) | data formatting | bytes 7176192 | tf_op jit(solution)/shard_map/reshape | solution.py:10
  329.4 5.0 %gather_fusion.1 = bf16[328,768]{1,0:T(8,128)(2,1)S(1)} fusion(bf16[768,2336]{0,1:T(8,128)(2,1)} %reshape.351, s32[1024]{0:T(1024)S(1)} %pad_clamp_fusion), kind=kCustom, calls=%fused_computation.1 | custom fusion | bytes 1008928 | tf_op jit(solution)/shard_map/jit(_take)/gather | solution.py:114
  334.4 8.4 %scatter_custom_fusion = f32[768,2048]{0,1:T(8,128)} fusion(f32[768,2048]{0,1:T(8,128)} %bitcast.1, s32[328]{0:T(512)S(1)} %reshape.370, f32[328]{0:T(512)S(1)} %get-tuple-element.66, bf16[328,768]{1,0:T(8,128)(2,1)S(1)} %gather_fusion.1, pred[328]{0:T(512)(128)(4,1)S(1)} %compare_and_fusion), kind=kCustom, calls=%fused_computation.31 | custom fusion | flops 1007616 | bytes 6797824 | tf_op jit(solution)/shard_map/scatter-add | solution.py:72
  342.8 8.4 %scatter_custom_fusion.1 = f32[768,2048]{0,1:T(8,128)} fusion(f32[768,2048]{0,1:T(8,128)} %scatter_custom_fusion, s32[328]{0:T(512)S(1)} %fusion.25, f32[328]{0:T(512)S(1)} %get-tuple-element.65, bf16[328,768]{1,0:T(8,128)(2,1)S(1)} %gather_fusion.1, pred[328]{0:T(512)(128)(4,1)S(1)} %compare_and_fusion), kind=kCustom, calls=%fused_computation.32 | custom fusion | flops 1007616 | bytes 6797824 | tf_op jit(solution)/shard_map/scatter-add | solution.py:72
  351.1 8.4 %scatter_custom_fusion.2 = f32[768,2048]{0,1:T(8,128)} fusion(f32[768,2048]{0,1:T(8,128)} %scatter_custom_fusion.1, s32[328]{0:T(512)S(1)} %fusion.26, f32[328]{0:T(512)S(1)} %get-tuple-element.64, bf16[328,768]{1,0:T(8,128)(2,1)S(1)} %gather_fusion.1, pred[328]{0:T(512)(128)(4,1)S(1)} %compare_and_fusion), kind=kCustom, calls=%fused_computation.33 | custom fusion | flops 1007616 | bytes 6797824 | tf_op jit(solution)/shard_map/scatter-add | solution.py:72
  359.5 8.5 %scatter_custom_fusion.3 = f32[768,2048]{0,1:T(8,128)} fusion(f32[768,2048]{0,1:T(8,128)} %scatter_custom_fusion.2, s32[328]{0:T(512)S(1)} %fusion.27, f32[328]{0:T(512)S(1)} %get-tuple-element.63, bf16[328,768]{1,0:T(8,128)(2,1)S(1)} %gather_fusion.1, pred[328]{0:T(512)(128)(4,1)S(1)} %compare_and_fusion), kind=kCustom, calls=%fused_computation.30 | custom fusion | flops 1007616 | bytes 6797824 | tf_op jit(solution)/shard_map/scatter-add | solution.py:72
  368.0 4.8 %convert_element_type.42 = bf16[768,2048]{0,1:T(8,128)(2,1)} convert(f32[768,2048]{0,1:T(8,128)} %scatter_custom_fusion.3) | non-fusion elementwise | flops 1572864 | bytes 9437184 | tf_op jit(solution)/shard_map/convert_element_type | solution.py:118
  372.8 5.0 %copy.14 = bf16[768,16,128]{2,1,0:T(8,128)(2,1)} copy(bf16[768,16,128]{0,2,1:T(8,128)(2,1)} %bitcast.57) | data formatting | bytes 6291456 | tf_op jit(solution)/shard_map/convert_element_type | solution.py:118
  (75 shorter events, 33.2 us)
Async XLA Ops:
  6.5 1.7 copy-start
  6.5 14.8 %copy-start.3 = (s32[1,8,41]{2,1,0:T(8,128)S(1)}, s32[1,8,41]{2,1,0:T(8,128)}, u32[]{:S(2)}) copy-start(s32[1,8,41]{2,1,0:T(8,128)} %param.14) | copy-start | bytes 3940
  6.5 14.9 %copy-start.2 = (f32[1,4,8,41]{3,2,1,0:T(8,128)S(1)}, f32[1,4,8,41]{3,2,1,0:T(8,128)}, u32[]{:S(2)}) copy-start(f32[1,4,8,41]{3,2,1,0:T(8,128)} %param.15) | copy-start | bytes 15748
  6.5 15.8 %copy-start.4 = (f32[768,9]{0,1:T(8,128)S(1)}, f32[768,9]{0,1:T(8,128)}, u32[]{:S(2)}) copy-start(f32[768,9]{0,1:T(8,128)} %param.12) | copy-start | bytes 82948
  6.5 86.7 %all-gather.3.cloned.1.call-start = ((), (), s32[]{:S(2)}) async-start(), calls=%async_computation.1 | async-start | bytes 5308416 | tf_op jit(solution)/shard_map/all_gather | solution.py:84
  9.1 166.0 %all-gather.5.cloned.1.call-start = ((), (), s32[]{:S(2)}) async-start(), calls=%async_computation.2 | async-start | bytes 15728640 | tf_op jit(solution)/shard_map/all_gather | solution.py:87
  14.0 231.7 %all-to-all-start = ((s32[8,1,41]{2,1,0:T(1,128)}), s32[8,1,41]{2,1,0:T(1,128)S(1)}, u32[]{:S(2)}, u32[]{:S(2)}) async-start(s32[8,1,41]{2,1,0:T(1,128)} %bitcast.2), calls=%async_computation | async-start | bytes 8192 | tf_op jit(solution)/shard_map/all_to_all | solution.py:107
  230.4 15.3 %collective-permute-start.2 = (bf16[768,292]{0,1:T(8,128)(2,1)S(1)}, bf16[768,292]{0,1:T(8,128)(2,1)S(1)}, u32[]{:S(2)}, u32[]{:S(2)}) collective-permute-start(bf16[768,292]{0,1:T(8,128)(2,1)S(1)} %pad_maximum_fusion), channel_id=1, source_target_pairs={{0,4},{4,8},{8,12},{12,16},{16,20},{20,24},{24,28},{28,0},{1,5},{5... | collective-permute-start | bytes 1345544 | tf_op jit(solution)/shard_map/ppermute | solution.py:20
  245.8 19.3 %collective-permute-start.3 = (bf16[768,292]{0,1:T(8,128)(2,1)S(1)}, bf16[768,292]{0,1:T(8,128)(2,1)S(1)}, u32[]{:S(2)}, u32[]{:S(2)}) collective-permute-start(bf16[768,292]{0,1:T(8,128)(2,1)S(1)} %collective-permute-done.2), channel_id=1, source_target_pairs={{0,4},{4,8},{8,12},{12,16},{16,20},{20,24},{24,28},{28,0},{1,5},{5... | collective-permute-start | bytes 1345544 | tf_op jit(solution)/shard_map/ppermute | solution.py:20
  246.0 31.4 %collective-permute-start.6 = (bf16[768,292]{0,1:T(8,128)(2,1)S(1)}, bf16[768,292]{0,1:T(8,128)(2,1)S(1)}, u32[]{:S(2)}, u32[]{:S(2)}) collective-permute-start(bf16[768,292]{0,1:T(8,128)(2,1)S(1)} %pad_maximum_fusion), channel_id=1, source_target_pairs={{4,0},{8,4},{12,8},{16,12},{20,16},{24,20},{28,24},{0,28},{5,1},{9... | collective-permute-start | bytes 1345544 | tf_op jit(solution)/shard_map/ppermute | solution.py:22
  265.1 27.3 %collective-permute-start.4 = (bf16[768,292]{0,1:T(8,128)(2,1)S(1)}, bf16[768,292]{0,1:T(8,128)(2,1)S(1)}, u32[]{:S(2)}, u32[]{:S(2)}) collective-permute-start(bf16[768,292]{0,1:T(8,128)(2,1)S(1)} %collective-permute-done.3), channel_id=1, source_target_pairs={{0,4},{4,8},{8,12},{12,16},{16,20},{20,24},{24,28},{28,0},{1,5},{5... | collective-permute-start | bytes 1345544 | tf_op jit(solution)/shard_map/ppermute | solution.py:20
  268.8 26.1 %collective-permute-start.1 = (bf16[768,1,128]{0,2,1:T(8,128)(2,1)S(1)}, bf16[768,1,128]{0,2,1:T(8,128)(2,1)S(1)}, u32[]{:S(2)}, u32[]{:S(2)}) collective-permute-start(bf16[768,1,128]{0,2,1:T(8,128)(2,1)S(1)} %get-tuple-element.45), channel_id=1, source_target_pairs={{4,0},{8,4},{12,8},{16,12},{20,16},{24,20},{28,24},{0,28},{5,1},{9... | collective-permute-start | bytes 589832 | tf_op jit(solution)/shard_map/ppermute | solution.py:38
  271.1 25.5 %collective-permute-start = (bf16[768,1,128]{0,2,1:T(8,128)(2,1)S(1)}, bf16[768,1,128]{0,2,1:T(8,128)(2,1)S(1)}, u32[]{:S(2)}, u32[]{:S(2)}) collective-permute-start(bf16[768,1,128]{0,2,1:T(8,128)(2,1)S(1)} %get-tuple-element.44), channel_id=1, source_target_pairs={{0,4},{4,8},{8,12},{12,16},{16,20},{20,24},{24,28},{28,0},{1,5},{5... | collective-permute-start | bytes 589832 | tf_op jit(solution)/shard_map/ppermute | solution.py:36
  277.4 29.5 %collective-permute-start.7 = (bf16[768,292]{0,1:T(8,128)(2,1)S(1)}, bf16[768,292]{0,1:T(8,128)(2,1)S(1)}, u32[]{:S(2)}, u32[]{:S(2)}) collective-permute-start(bf16[768,292]{0,1:T(8,128)(2,1)S(1)} %collective-permute-done.6), channel_id=1, source_target_pairs={{4,0},{8,4},{12,8},{16,12},{20,16},{24,20},{28,24},{0,28},{5,1},{9... | collective-permute-start | bytes 1345544 | tf_op jit(solution)/shard_map/ppermute | solution.py:22
  292.4 14.5 %collective-permute-start.5 = (bf16[768,292]{0,1:T(8,128)(2,1)S(1)}, bf16[768,292]{0,1:T(8,128)(2,1)S(1)}, u32[]{:S(2)}, u32[]{:S(2)}) collective-permute-start(bf16[768,292]{0,1:T(8,128)(2,1)S(1)} %collective-permute-done.4), channel_id=1, source_target_pairs={{0,4},{4,8},{8,12},{12,16},{16,20},{20,24},{24,28},{28,0},{1,5},{5... | collective-permute-start | bytes 1345544 | tf_op jit(solution)/shard_map/ppermute | solution.py:20
  306.9 12.4 %collective-permute-start.8 = (bf16[768,292]{0,1:T(8,128)(2,1)S(1)}, bf16[768,292]{0,1:T(8,128)(2,1)S(1)}, u32[]{:S(2)}, u32[]{:S(2)}) collective-permute-start(bf16[768,292]{0,1:T(8,128)(2,1)S(1)} %collective-permute-done.7), channel_id=1, source_target_pairs={{4,0},{8,4},{12,8},{16,12},{20,16},{24,20},{28,24},{0,28},{5,1},{9... | collective-permute-start | bytes 1345544 | tf_op jit(solution)/shard_map/ppermute | solution.py:22
  359.5 18.3 %copy-start.1 = (bf16[3072,384]{1,0:T(8,128)(2,1)S(1)}, bf16[3072,384]{1,0:T(8,128)(2,1)}, u32[]{:S(2)}) copy-start(bf16[3072,384]{1,0:T(8,128)(2,1)} %param.11) | copy-start | bytes 7077892
Sparse Core Ops, SparseCore 0:
  9.4 83.7 all-gather.2
  94.8 80.2 all-gather.4
